TPU v7x, 512 devices: a whole 4x4x16 slice. The times are simulated.
512 devices in a mesh: ctx: 16 (over x, y), clu: 32 (over z, core).
Axes of the slice: x: 4, y: 4, z: 16, core: 2. Of those that a mesh axis runs over, the one named last changes fastest.
Arguments:
- queries: bfloat16 [131072, 1024], P(('ctx', 'clu')), may hold values from -6 to 6
- keys: bfloat16 [131072, 1024], P(('ctx', 'clu')), may hold values from -6 to 6
- values: bfloat16 [131072, 1024], P(('ctx', 'clu')), may hold values from -6 to 6
- clusters: int32 [131072, 8], P(('ctx', 'clu')), may hold values from 0 to 511, as said below
- centroids: float32 [512, 8, 128], P('clu'), may hold values from -0.5 to 0.5
Outputs:
- attended: bfloat16 [131072, 1024], P(('ctx', 'clu'))
- new_centroids: float32 [512, 8, 128], replicated
Inputs may be any that keep to these rules, and one draw needn't show every extreme that they name: For each head, the 256 rows of one device name clusters of any one owner (clusters o * 16 to (o + 1) * 16 - 1) at most 32 times, and those of some owner exactly 32 times.
All inputs are finite; a program needn't handle non-finite values.
Results may differ from a plain program's by a relative error of at most 0.018.
Values may be sent and summed in bfloat16 or wider, within the bound.
A program may use at most 64 MiB of HBM per device.

v0:
```python
import math

import jax
import jax.numpy as jnp
from jax import lax
from jax.sharding import PartitionSpec as P

CAP = 32


EPS = 1e-06
SCALE = 8.0
DECAY = 0.75


def unit_rows(rows):
    floats = rows.astype(jnp.float32)
    factor = lax.rsqrt(jnp.mean(floats * floats, axis=-1, keepdims=True) + EPS) / math.sqrt(
        floats.shape[-1]
    )
    return (floats * factor).astype(jnp.bfloat16)


def pack_rows(queries, keys, values, clusters, n_owner, cap, c_dev):
    tok_count, head_count = clusters.shape
    head_size = queries.shape[1] // head_count
    query_rows = unit_rows(queries.reshape(tok_count, head_count, head_size))
    key_rows = unit_rows(keys.reshape(tok_count, head_count, head_size))
    value_rows = values.reshape(tok_count, head_count, head_size)
    owners = clusters // c_dev
    member = clusters % c_dev
    onehot = (owners[:, :, None] == jnp.arange(n_owner, dtype=jnp.int32)[None, None, :]).astype(
        jnp.int32
    )
    slot_rank = jnp.sum((jnp.cumsum(onehot, axis=0) - onehot) * onehot, axis=-1)
    head_idx = jnp.broadcast_to(
        jnp.arange(head_count, dtype=jnp.int32)[None, :], (tok_count, head_count)
    )
    tok_idx = jnp.broadcast_to(
        jnp.arange(tok_count, dtype=jnp.int32)[:, None], (tok_count, head_count)
    )

    def place(rows):
        return (
            jnp.zeros((n_owner, head_count, cap, head_size), jnp.bfloat16)
            .at[owners, head_idx, slot_rank]
            .set(rows)
        )

    codes = (
        jnp.zeros((n_owner, head_count, cap), jnp.int32)
        .at[owners, head_idx, slot_rank]
        .set(tok_idx * (c_dev + 1) + member + 1)
    )
    return (
        (place(query_rows), place(key_rows), place(value_rows), codes),
        owners,
        head_idx,
        slot_rank,
    )


def attend_one(query_slots, key_slots, value_slots, meta_slots, tok_dev, c_dev):
    n_source, cap, head_size = query_slots.shape
    total_rows = n_source * cap
    query_rows = query_slots.reshape(total_rows, head_size)
    key_rows = key_slots.reshape(total_rows, head_size)
    value_rows = value_slots.reshape(total_rows, head_size)
    codes = meta_slots.reshape(total_rows)
    member = codes % (c_dev + 1)
    position = jnp.arange(total_rows, dtype=jnp.int32) // cap * tok_dev + codes // (c_dev + 1)
    scores = jnp.dot(query_rows, key_rows.T, preferred_element_type=jnp.float32) * SCALE
    allowed = (member[:, None] == member[None, :]) & (position[None, :] <= position[:, None])
    weights = jnp.where(allowed, jnp.exp(scores), jnp.float32(0.0))
    probs = (weights / jnp.sum(weights, axis=-1, keepdims=True)).astype(jnp.bfloat16)
    mixed = jnp.dot(probs, value_rows, preferred_element_type=jnp.float32).astype(jnp.bfloat16)
    selector = (member[None, :] == jnp.arange(1, c_dev + 1, dtype=jnp.int32)[:, None]).astype(
        jnp.bfloat16
    )
    sums = jnp.dot(selector, query_rows, preferred_element_type=jnp.float32) + jnp.dot(
        selector, key_rows, preferred_element_type=jnp.float32
    )
    return (mixed.reshape(n_source, cap, head_size), sums)


def attend_heads(query_slots, key_slots, value_slots, meta_slots, tok_dev, c_dev):

    def per_head(items):
        return attend_one(items[0], items[1], items[2], items[3], tok_dev, c_dev)

    mixed, sums = lax.map(
        per_head,
        (
            jnp.moveaxis(query_slots, 1, 0),
            jnp.moveaxis(key_slots, 1, 0),
            jnp.moveaxis(value_slots, 1, 0),
            jnp.moveaxis(meta_slots, 1, 0),
        ),
    )
    return (jnp.moveaxis(mixed, 0, 1), jnp.moveaxis(sums, 0, 1))


def local(queries, keys, values, clusters, centroids):
    n_owner = lax.axis_size("clu")
    tok_dev = queries.shape[0]
    c_dev = centroids.shape[0]
    packed, owners, head_idx, slot_rank = pack_rows(
        queries, keys, values, clusters, n_owner, CAP, c_dev
    )
    arrived = (
        lax.all_to_all(packed[0], "clu", split_axis=0, concat_axis=0, tiled=True),
        lax.all_to_all(packed[1], "clu", split_axis=0, concat_axis=0, tiled=True),
        lax.all_to_all(packed[2], "clu", split_axis=0, concat_axis=0, tiled=True),
        lax.all_to_all(packed[3], "clu", split_axis=0, concat_axis=0, tiled=True),
    )
    mixed, sums = attend_heads(arrived[0], arrived[1], arrived[2], arrived[3], tok_dev, c_dev)
    back = lax.all_to_all(mixed, "clu", split_axis=0, concat_axis=0, tiled=True)
    attended = back[owners, head_idx, slot_rank].reshape(tok_dev, queries.shape[1])
    total = lax.psum(sums.astype(jnp.bfloat16), "ctx").astype(jnp.float32)
    fresh = DECAY * centroids + (1.0 - DECAY) / 2.0 * total
    gathered = lax.all_gather(fresh, "clu", axis=0, tiled=True)
    return (attended, gathered)


def solution(mesh):
    placed = (
        P(("ctx", "clu"), None),
        P(("ctx", "clu"), None),
        P(("ctx", "clu"), None),
        P(("ctx", "clu"), None),
        P("clu", None, None),
    )
    return jax.shard_map(
        local, mesh=mesh, in_specs=placed, out_specs=(P(("ctx", "clu"), None), P()), check_vma=False
    )
```

profile of v0, /device:TPU:1, one launch (start us, length us, event | category | flops | bytes accessed | tf_op | source)
XLA Modules:
  0.0 603.9 jit_solution(9892113824945366414)
XLA Ops:
  7.2 0.8 fusion.36
  8.3 18.0 %reduce-window.6 = s32[32,8,2,128]{3,1,2,0:T(8,128)S(1)} reduce-window(s32[32,8,2,128]{3,1,2,0:T(8,128)S(1)} %fusion.31, s32[]{:T(128)} %constant.143.clone.1), window={size=1x1x1x128 pad=0_0x0_0x0_0x127_0}, to_apply=%region_0.0 | reduce-window | flops 8323072 | bytes 524292 | tf_op jit(solution)/shard_map/reduce-window
  27.4 8.1 %scatter_custom_fusion = s32[8192]{0:T(1024)S(1)} fusion(s32[2048]{0:T(1024)S(1)} %reshape.244, s32[2048]{0:T(1024)S(1)} %reshape.246, s32[]{:T(128)} %constant.143.clone.1), kind=kCustom, calls=%fused_computation.70 | custom fusion | bytes 32772
  36.3 16.7 %all-to-all-start = ((s32[32,1,256]{2,1,0:T(1,128)}), s32[32,1,256]{2,1,0:T(1,128)S(1)}, u32[]{:S(2)}, u32[]{:S(2)}) async-start(s32[32,1,256]{2,1,0:T(1,128)} %reshape.278), calls=%async_computation | async-start | bytes 65536 | tf_op jit(solution)/shard_map/all_to_all | solution.py:114
  53.9 7.8 %scatter_custom_fusion.1 = bf16[8192,128]{1,0:T(8,128)(2,1)} fusion(s32[2048]{0:T(1024)S(1)} %reshape.244, bf16[]{:T(256)} %constant.144.clone.1, f32[256,8,128]{2,1,0:T(8,128)S(1)} %bitcast.95, f32[256,8]{1,0:T(8,128)S(1)} %copy.50), kind=kCustom, calls=%fused_computation.47 | custom fusion | flops 524288 | bytes 3276802
  61.7 3.4 all-to-all-done
  65.1 8.9 %all-to-all-start.1 = ((bf16[32,8,32,128]{3,2,1,0:T(8,128)(2,1)}), bf16[32,8,32,128]{3,2,1,0:T(8,128)(2,1)S(1)}, u32[]{:S(2)}, u32[]{:S(2)}) async-start(bf16[32,8,32,128]{3,2,1,0:T(8,128)(2,1)} %bitcast.14), calls=%async_computation.1 | async-start | bytes 4194304 | tf_op jit(solution)/shard_map/all_to_all | solution.py:111
  75.0 7.8 %scatter_custom_fusion.2 = bf16[8192,128]{1,0:T(8,128)(2,1)} fusion(s32[2048]{0:T(1024)S(1)} %reshape.244, bf16[]{:T(256)} %constant.144.clone.1, f32[256,8,128]{2,1,0:T(8,128)S(1)} %bitcast.97, f32[256,8]{1,0:T(8,128)S(1)} %copy.52), kind=kCustom, calls=%fused_computation.45 | custom fusion | flops 524288 | bytes 3276802
  82.8 89.9 %all-to-all-done.1 = bf16[32,8,32,128]{3,2,1,0:T(8,128)(2,1)S(1)} async-done(((bf16[32,8,32,128]{3,2,1,0:T(8,128)(2,1)}), bf16[32,8,32,128]{3,2,1,0:T(8,128)(2,1)S(1)}, u32[]{:S(2)}, u32[]{:S(2)}) %all-to-all-start.1) | async-done | bytes 2097184 | tf_op jit(solution)/shard_map/all_to_all | solution.py:111
  172.7 5.3 all-to-all-start.2
  178.3 7.4 %scatter_custom_fusion.3 = bf16[8192,128]{1,0:T(8,128)(2,1)} fusion(s32[2048]{0:T(1024)S(1)} %reshape.244, bf16[2048,128]{1,0:T(8,128)(2,1)S(1)} %reshape.264, bf16[]{:T(256)} %constant.144.clone.1), kind=kCustom, calls=%fused_computation.43 | custom fusion | bytes 2097154
  185.7 91.6 %all-to-all-done.2 = bf16[32,8,32,128]{3,2,1,0:T(8,128)(2,1)} async-done(((bf16[32,8,32,128]{3,2,1,0:T(8,128)(2,1)}), bf16[32,8,32,128]{3,2,1,0:T(8,128)(2,1)}, u32[]{:S(2)}, u32[]{:S(2)}) %all-to-all-start.2) | async-done | bytes 2097184 | tf_op jit(solution)/shard_map/all_to_all | solution.py:112
  277.3 6.9 %all-to-all-start.3 = ((bf16[32,8,32,128]{3,2,1,0:T(8,128)(2,1)}), bf16[32,8,32,128]{3,2,1,0:T(8,128)(2,1)}, u32[]{:S(2)}, u32[]{:S(2)}) async-start(bf16[32,8,32,128]{3,2,1,0:T(8,128)(2,1)} %bitcast.19), calls=%async_computation.3 | async-start | bytes 4194304 | tf_op jit(solution)/shard_map/all_to_all | solution.py:113
  285.5 97.9 %all-to-all-done.3 = bf16[32,8,32,128]{3,2,1,0:T(8,128)(2,1)} async-done(((bf16[32,8,32,128]{3,2,1,0:T(8,128)(2,1)}), bf16[32,8,32,128]{3,2,1,0:T(8,128)(2,1)}, u32[]{:S(2)}, u32[]{:S(2)}) %all-to-all-start.3) | async-done | bytes 2097184 | tf_op jit(solution)/shard_map/all_to_all | solution.py:113
  383.4 45.1 %while.15 = (s32[]{:T(128)}, bf16[8,32,32,128]{3,2,0,1:T(8,128)(2,1)}, bf16[8,16,128]{2,0,1:T(8,128)(2,1)S(1)}, s32[8,32,32]{2,0,1:T(8,128)S(1)}, bf16[8,32,32,1...) while((s32[]{:T(128)}, ...), condition=%wide.region_11.12_spmd, body=%wide.region_9.11_spmd.sunk | while | flops 559078400 | bytes 12194105 | solution.py:91
  383.9 1.1 constant_dynamic-slice_fusion.7
  385.2 1.3 fusion.63
  386.6 1.7 fusion.64
  388.3 0.8 constant_dynamic-update-slice_fusion.2
  389.5 1.1 constant_dynamic-slice_fusion.7
  390.9 1.3 fusion.63
  392.2 1.7 fusion.64
  395.2 1.1 constant_dynamic-slice_fusion.7
  396.5 1.3 fusion.63
  397.8 1.7 fusion.64
  399.6 0.8 constant_dynamic-update-slice_fusion.2
  400.8 1.1 constant_dynamic-slice_fusion.7
  402.2 1.3 fusion.63
  403.5 1.7 fusion.64
  405.2 0.8 constant_dynamic-update-slice_fusion.2
  406.5 1.1 constant_dynamic-slice_fusion.7
  407.8 1.3 fusion.63
  409.1 1.7 fusion.64
  412.1 1.1 constant_dynamic-slice_fusion.7
  413.5 1.3 fusion.63
  414.8 1.7 fusion.64
  417.8 1.1 constant_dynamic-slice_fusion.7
  419.1 1.3 fusion.63
  420.4 1.7 fusion.64
  423.4 1.1 constant_dynamic-slice_fusion.7
  424.7 1.3 fusion.63
  426.1 1.7 fusion.64
  428.5 6.5 %all-to-all-start.4 = ((bf16[32,8,32,128]{3,2,1,0:T(8,128)(2,1)}), bf16[32,8,32,128]{3,2,1,0:T(8,128)(2,1)S(1)}, u32[]{:S(2)}, u32[]{:S(2)}) async-start(bf16[32,8,32,128]{3,2,1,0:T(8,128)(2,1)} %bitcast.107), calls=%async_computation.4 | async-start | bytes 4194304 | tf_op jit(solution)/shard_map/all_to_all | solution.py:117
  435.0 63.7 %psum.7 = bf16[16,8,128]{2,1,0:T(8,128)(2,1)S(1)} all-reduce(bf16[16,8,128]{2,1,0:T(8,128)(2,1)S(1)} %bitcast.111), channel_id=1, replica_groups=mesh['ctx'=16,'clu'=32] {'ctx'}, use_global_device_ids=true, to_apply=%region_12.13 | all-reduce | flops 16384 | bytes 65536 | tf_op jit(solution)/shard_map/psum | solution.py:119
  499.6 80.0 %all-gather.2.cloned.1.call-done = f32[512,8,128]{2,1,0:T(8,128)} async-done(((f32[16,8,128]{2,1,0:T(8,128)}), f32[512,8,128]{2,1,0:T(8,128)}) %all-gather.2.cloned.1.call-update) | async-done | bytes 2097168 | tf_op jit(solution)/shard_map/all_gather | solution.py:121
  579.6 13.4 %gather_fusion = bf16[2048,128]{1,0:T(8,128)(2,1)S(1)} fusion(bf16[32,8,32,128]{3,2,1,0:T(8,128)(2,1)S(1)} %all-to-all-done.4, s32[2048]{0:T(1024)S(1)} %reshape.238), kind=kCustom, calls=%fused_computation | custom fusion | bytes 1073152 | tf_op jit(solution)/shard_map/gather | solution.py:118
  593.0 1.0 reshape.219
  594.0 3.0 copy.84
  (156 shorter events, 16.0 us)
Async XLA Ops:
  7.2 19.8 %copy-start.5 = (s32[3]{0:T(128)S(1)}, s32[3]{0:T(128)}, u32[]{:S(2)}) copy-start(s32[3]{0:T(128)} %constant.166) | copy-start | bytes 40
  7.2 19.8 %copy-start.4 = (s32[3]{0:T(128)S(1)}, s32[3]{0:T(128)}, u32[]{:S(2)}) copy-start(s32[3]{0:T(128)} %constant.163) | copy-start | bytes 40
  7.2 45.8 %copy-start = (bf16[256,1024]{1,0:T(8,128)(2,1)S(1)}, bf16[256,1024]{1,0:T(8,128)(2,1)}, u32[]{:S(2)}) copy-start(bf16[256,1024]{1,0:T(8,128)(2,1)} %param.7) | copy-start | bytes 1572868
  36.3 28.9 %all-to-all-start = ((s32[32,1,256]{2,1,0:T(1,128)}), s32[32,1,256]{2,1,0:T(1,128)S(1)}, u32[]{:S(2)}, u32[]{:S(2)}) async-start(s32[32,1,256]{2,1,0:T(1,128)} %reshape.278), calls=%async_computation | async-start | bytes 65536 | tf_op jit(solution)/shard_map/all_to_all | solution.py:114
  65.1 8.9 %copy-start.1 = (bf16[256,1024]{1,0:T(8,128)(2,1)S(1)}, bf16[256,1024]{1,0:T(8,128)(2,1)}, u32[]{:S(2)}) copy-start(bf16[256,1024]{1,0:T(8,128)(2,1)} %param.8) | copy-start | bytes 1572868
  65.1 107.5 %all-to-all-start.1 = ((bf16[32,8,32,128]{3,2,1,0:T(8,128)(2,1)}), bf16[32,8,32,128]{3,2,1,0:T(8,128)(2,1)S(1)}, u32[]{:S(2)}, u32[]{:S(2)}) async-start(bf16[32,8,32,128]{3,2,1,0:T(8,128)(2,1)} %bitcast.14), calls=%async_computation.1 | async-start | bytes 4194304 | tf_op jit(solution)/shard_map/all_to_all | solution.py:111
  172.7 5.4 copy-start.2
  172.7 104.6 %all-to-all-start.2 = ((bf16[32,8,32,128]{3,2,1,0:T(8,128)(2,1)}), bf16[32,8,32,128]{3,2,1,0:T(8,128)(2,1)}, u32[]{:S(2)}, u32[]{:S(2)}) async-start(bf16[32,8,32,128]{3,2,1,0:T(8,128)(2,1)} %bitcast.17), calls=%async_computation.2 | async-start | bytes 4194304 | tf_op jit(solution)/shard_map/all_to_all | solution.py:112
  277.3 106.1 %all-to-all-start.3 = ((bf16[32,8,32,128]{3,2,1,0:T(8,128)(2,1)}), bf16[32,8,32,128]{3,2,1,0:T(8,128)(2,1)}, u32[]{:S(2)}, u32[]{:S(2)}) async-start(bf16[32,8,32,128]{3,2,1,0:T(8,128)(2,1)} %bitcast.19), calls=%async_computation.3 | async-start | bytes 4194304 | tf_op jit(solution)/shard_map/all_to_all | solution.py:113
  428.5 70.2 %copy-start.3 = (f32[16,8,128]{2,1,0:T(8,128)S(1)}, f32[16,8,128]{2,1,0:T(8,128)}, u32[]{:S(2)}) copy-start(f32[16,8,128]{2,1,0:T(8,128)} %param.11) | copy-start | bytes 196612
  428.5 151.1 %all-to-all-start.4 = ((bf16[32,8,32,128]{3,2,1,0:T(8,128)(2,1)}), bf16[32,8,32,128]{3,2,1,0:T(8,128)(2,1)S(1)}, u32[]{:S(2)}, u32[]{:S(2)}) async-start(bf16[32,8,32,128]{3,2,1,0:T(8,128)(2,1)} %bitcast.107), calls=%async_computation.4 | async-start | bytes 4194304 | tf_op jit(solution)/shard_map/all_to_all | solution.py:117
  435.0 144.6 %all-gather.2.cloned.1.call-start = ((), (), s32[]{:S(2)}) async-start(), calls=%async_computation.5 | async-start | bytes 2162688 | tf_op jit(solution)/shard_map/all_gather | solution.py:121
Sparse Core Ops, SparseCore 0:
  499.5 80.0 all-gather.1
where the time goes:
time: 605 us; the launch traced here: 604 us
  waiting for transfers between devices  363 us (60%)
  blocking collectives  63.7 us (11%)
  local copies, waits for them, and re-layouts  53.7 us (9%)
  starting transfers between devices  44.4 us (7%)
  other arithmetic  37.2 us (6%)
  matrix products  27.3 us (5%)
  between operations  14.4 us (2%)
    all_to_all x1, waiting for transfers between devices, local(): lax.all_to_all(packed[2], 'clu', split_axis=0, concat_axis=0, tiled=True)  97.9 us
    all_to_all x1, waiting for transfers between devices, local(): lax.all_to_all(packed[1], 'clu', split_axis=0, concat_axis=0, tiled=True)  91.6 us
    all_to_all x1, waiting for transfers between devices, local(): lax.all_to_all(packed[0], 'clu', split_axis=0, concat_axis=0, tiled=True)  89.9 us
    all_gather x1, waiting for transfers between devices, local(): gathered = lax.all_gather(fresh, 'clu', axis=0, tiled=True)  80 us
    psum x1, blocking collectives, local(): total = lax.psum(sums.astype(jnp.bfloat16), 'ctx').astype(jnp.float32)  63.7 us
    unnamed x21, local copies, waits for them, and re-layouts  20 us
    another operation x2, other arithmetic  18.1 us
    all_to_all x1, starting transfers between devices, local(): lax.all_to_all(packed[3], 'clu', split_axis=0, concat_axis=0, tiled=True)  16.7 us
  transfers between devices with their start and end apart: 6, of which 5 were waited for; matrix products, arithmetic and copies ran while one was open for 4% of the time, Pallas kernels for 0%

commit v1 on v0

v1 whole, which is shorter than its diff:
```python
import functools
import math

import jax
import jax.numpy as jnp
from jax import lax
from jax.experimental import pallas as pl
from jax.experimental.pallas import tpu as pltpu
from jax.sharding import PartitionSpec as P

MESH = pl.DeviceIdType.MESH
EPS = 1e-06
SCALE = 8.0
DECAY = 0.75
D = 128
GAP = 64.0

BF = jnp.bfloat16
F32 = jnp.float32


def unit(rows):
    factor = lax.rsqrt(jnp.mean(rows * rows, axis=-1, keepdims=True) + EPS) / math.sqrt(D)
    return (rows * factor).astype(BF)


def kernel(
    n_ctx,
    n_clu,
    q_ref,
    k_ref,
    v_ref,
    clt_ref,
    cent_ref,
    out_ref,
    newc_ref,
    kst,
    nrm,
    kbuf,
    vbuf,
    qbuf,
    obuf,
    acc,
    sst,
    sin,
    zst,
    zin,
    fin,
    vs,
    vr,
    ks,
    kr,
    qs,
    qr,
    vfs,
    vfr,
    kfs,
    kfr,
    os_,
    or_,
    xs,
    xr,
    zs,
    zr,
    fs,
    fr,
    gs,
    gr,
):
    tok = q_ref.shape[0]
    heads = q_ref.shape[1] // D
    n_z = n_clu // 2
    step = n_z // heads
    bits = max(1, (n_ctx * n_clu - 1).bit_length())

    col = lax.axis_index("ctx")
    me = lax.axis_index("clu")
    z = me // 2
    core = lax.rem(me, 2)
    sib = (col, me + 1 - 2 * core)
    is_home = lax.rem(z, step) == 0
    my_head = z // step

    def spread(i, base, n):
        off = jnp.where(lax.rem(i, 2) == 1, (i + 1) // 2, n - i // 2)
        return lax.rem(base + off, n)

    def remote(src, dst, send, recv, dev):
        return pltpu.make_async_remote_copy(
            src_ref=src, dst_ref=dst, send_sem=send, recv_sem=recv, device_id=dev, device_id_type=MESH
        )

    def lanes(h):
        return pl.ds(pl.multiple_of(h * D, D), D)

    barrier = pltpu.get_barrier_semaphore()

    def greet_clu(i, c):
        pl.semaphore_signal(barrier, inc=1, device_id=(col, lax.rem(me + i, n_clu)), device_id_type=MESH)
        return c

    def greet_ctx(i, c):
        pl.semaphore_signal(barrier, inc=1, device_id=(lax.rem(col + i, n_ctx), me), device_id_type=MESH)
        return c

    lax.fori_loop(1, n_clu, greet_clu, 0)
    lax.fori_loop(1, n_ctx, greet_ctx, 0)
    pl.semaphore_wait(barrier, n_clu - 1 + n_ctx - 1)

    def v_src(h):
        return v_ref.at[:, lanes(h)]

    def q_src(h):
        return nrm.at[h, :, pl.ds(0, D)]

    def v_dst(c):
        return vbuf.at[c, :, pl.ds(0, D)]

    def k_dst(c):
        return kbuf.at[c, pl.ds(0, D + 16), :]

    def to_home(h, src, dst, send, recv):
        target = h * step

        @pl.when(target == z)
        def _():
            pltpu.make_async_copy(src, dst, recv.at[z]).start()

        @pl.when(target != z)
        def _():
            remote(src, dst, send.at[h], recv.at[z], (col, target * 2 + core)).start()

    def sent_home(h, src, dst, send, recv):
        target = h * step

        @pl.when(target != z)
        def _():
            remote(src, dst, send.at[h], recv.at[z], (col, target * 2 + core)).wait_send()

    def send_v(i, c):
        h = spread(i, z // step, heads)
        to_home(h, v_src(h), v_dst(me), vs, vr)
        return c

    lax.fori_loop(0, heads, send_v, 0)

    row_id = lax.broadcasted_iota(jnp.int32, (16, tok), 0)

    def send_k(i, c):
        h = spread(i, z // step, heads)
        kn = unit(k_ref[:, lanes(h)].astype(F32))
        qn = unit(q_ref[:, lanes(h)].astype(F32))
        nrm[h, :, pl.ds(0, D)] = qn
        nrm[h, :, pl.ds(D, D)] = kn
        kst[h, pl.ds(0, D), :] = jnp.transpose(kn.astype(F32)).astype(BF)
        ids = clt_ref[pl.ds(h, 1), :]
        code = 2 * (lax.shift_right_logical(jnp.broadcast_to(ids, (16, tok)), row_id) & 1) - 1
        code = jnp.where(row_id < bits, code, jnp.where(row_id == bits, 1, 0))
        kst[h, pl.ds(D, 16), :] = code.astype(F32).astype(BF)
        to_home(h, kst.at[h], k_dst(me), ks, kr)
        return c

    lax.fori_loop(0, heads, send_k, 0)

    def send_q(i, c):
        h = spread(i, z // step, heads)
        to_home(h, q_src(h), qbuf.at[z], qs, qr)
        return c

    lax.fori_loop(0, heads, send_q, 0)

    n_row = n_ctx * n_clu
    sum_row = lax.broadcasted_iota(jnp.int32, (n_row, tok), 0)

    def sum_head(h, c):
        ids = clt_ref[pl.ds(h, 1), :]
        place = lax.rem(ids, n_ctx) * n_clu + ids // n_ctx
        pick = jnp.where(sum_row == place, 1.0, 0.0).astype(BF)
        both = jnp.dot(pick, nrm[h], preferred_element_type=F32)
        both = both[:, :D] + both[:, D:]
        sst[:, h, :, :] = both.reshape(n_ctx, n_clu, D).astype(BF)
        return c

    lax.fori_loop(0, heads, sum_head, 0)

    def x_copy(c):
        return remote(sst.at[c], sin.at[col], xs.at[c], xr.at[col], (c, me))

    def x_start(i, c):
        x_copy(lax.rem(col + i, n_ctx)).start()
        return c

    lax.fori_loop(1, n_ctx, x_start, 0)
    sin[col] = sst[col]

    @pl.when(is_home)
    def _():
        def fill(c, carry):
            vbuf[c, :, pl.ds(D, D)] = jnp.ones((tok, D), BF)
            kbuf[c, pl.ds(D + 16, D - 16), :] = jnp.zeros((D - 16, tok), BF)
            return carry

        lax.fori_loop(0, n_clu, fill, 0)

    def x_wait(i, c):
        other = lax.rem(col + i, n_ctx)
        pltpu.make_async_copy(sin.at[other], sin.at[other], xr.at[other]).wait()
        return c

    lax.fori_loop(1, n_ctx, x_wait, 0)
    for h in range(heads):
        part = sin[0, h].astype(F32)
        for c in range(1, n_ctx):
            part = part + sin[c, h].astype(F32)
        zst[pl.ds(h, n_clu, stride=heads), :] = part

    def z_src(o):
        return zst.at[pl.ds(pl.multiple_of(o * heads, heads), heads), :]

    def z_copy(o):
        return remote(z_src(o), zin.at[me], zs.at[o], zr.at[me], (col, o))

    def z_start(i, c):
        z_copy(lax.rem(me + i, n_clu)).start()
        return c

    lax.fori_loop(1, n_clu, z_start, 0)
    zin[me] = zst[pl.ds(pl.multiple_of(me * heads, heads), heads), :]

    def z_wait(i, c):
        o = lax.rem(me + i, n_clu)
        pltpu.make_async_copy(zin.at[o], zin.at[o], zr.at[o]).wait()
        return c

    lax.fori_loop(1, n_clu, z_wait, 0)
    total = jnp.sum(zin[...], axis=0)
    fin[me] = DECAY * cent_ref[col] + (1.0 - DECAY) / 2.0 * total

    def f_copy(o):
        return remote(fin.at[me], fin.at[me], fs.at[o], fr.at[me], (col, o))

    def f_start(i, c):
        f_copy(lax.rem(me + i, n_clu)).start()
        return c

    lax.fori_loop(1, n_clu, f_start, 0)

    def f_wait(i, c):
        o = lax.rem(me + i, n_clu)
        pltpu.make_async_copy(fin.at[o], fin.at[o], fr.at[o]).wait()
        return c

    lax.fori_loop(1, n_clu, f_wait, 0)

    def g_copy(c):
        return remote(fin, newc_ref.at[:, col], gs.at[c], gr.at[col], (c, me))

    def g_start(i, c):
        g_copy(lax.rem(col + i, n_ctx)).start()
        return c

    lax.fori_loop(1, n_ctx, g_start, 0)
    own_fresh = pltpu.make_async_copy(fin, newc_ref.at[:, col], gr.at[col])
    own_fresh.start()

    def v_pass(t):
        c = 2 * t + core
        return remote(v_dst(c), v_dst(c), vfs.at[t], vfr.at[t], sib)

    def k_pass(t):
        c = 2 * t + core
        return remote(k_dst(c), k_dst(c), kfs.at[t], kfr.at[t], sib)

    def out_dst(h):
        return out_ref.at[:, lanes(h)]

    def o_copy(t):
        return remote(obuf.at[t], out_dst(my_head), os_.at[t], or_.at[my_head], (col, 2 * t + core))

    def own_copy():
        return pltpu.make_async_copy(obuf.at[z], out_dst(my_head), or_.at[my_head])

    @pl.when(is_home)
    def _():
        def pass_v(i, c):
            t = spread(i, z, n_z)
            pltpu.make_async_copy(v_dst(2 * t + core), v_dst(2 * t + core), vr.at[t]).wait()
            v_pass(t).start()
            return c

        lax.fori_loop(0, n_z, pass_v, 0)

        def pass_k(i, c):
            t = spread(i, z, n_z)
            pltpu.make_async_copy(k_dst(2 * t + core), k_dst(2 * t + core), kr.at[t]).wait()
            k_pass(t).start()
            return c

        lax.fori_loop(0, n_z, pass_k, 0)

        def arrive(i, c):
            t = spread(i, z, n_z)
            o = 2 * t + 1 - core
            pltpu.make_async_copy(v_dst(o), v_dst(o), vfr.at[t]).wait()
            pltpu.make_async_copy(k_dst(o), k_dst(o), kfr.at[t]).wait()
            return c

        lax.fori_loop(0, n_z, arrive, 0)

        lane = lax.broadcasted_iota(jnp.int32, (tok, D), 1)
        weight = jnp.where(lane < bits, GAP, jnp.where(lane == bits, -GAP * bits, 0.0))
        key_at = lax.broadcasted_iota(jnp.int32, (tok, tok), 1)
        query_at = lax.broadcasted_iota(jnp.int32, (tok, tok), 0) + core * tok

        def attend(i, carry):
            t = spread(i, z, n_z)
            pltpu.make_async_copy(qbuf.at[t], qbuf.at[t], qr.at[t]).wait()
            mine = qbuf[t].astype(F32) * SCALE
            code = jnp.transpose(kbuf[2 * t + core, pl.ds(D, D), :].astype(F32)) * weight
            query = jnp.concatenate([mine, code], axis=1).astype(BF)

            def scores(c):
                return jnp.exp(jnp.dot(query, kbuf[c], preferred_element_type=F32))

            def mix(p, c):
                return jnp.dot(p.astype(BF), vbuf[c], preferred_element_type=F32)

            p0 = jnp.where(key_at <= query_at, scores(2 * t), 0.0)
            p1 = jnp.where(key_at + tok <= query_at, scores(2 * t + 1), 0.0)
            acc[...] = mix(p0, 2 * t) + mix(p1, 2 * t + 1)

            def earlier(u, c):
                acc[...] += mix(scores(2 * u), 2 * u) + mix(scores(2 * u + 1), 2 * u + 1)
                return c

            lax.fori_loop(0, t, earlier, 0)
            obuf[t] = (acc[:, pl.ds(0, D)] / acc[:, pl.ds(D, D)]).astype(BF)

            @pl.when(t == z)
            def _():
                own_copy().start()

            @pl.when(t != z)
            def _():
                o_copy(t).start()

            return carry

        lax.fori_loop(0, n_z, attend, 0)

        def done(i, c):
            t = lax.rem(z + i, n_z)
            v_pass(t).wait_send()
            k_pass(t).wait_send()

            @pl.when(t != z)
            def _():
                o_copy(t).wait_send()

            return c

        lax.fori_loop(0, n_z, done, 0)

    def o_wait(h, c):
        pltpu.make_async_copy(out_dst(h), out_dst(h), or_.at[h]).wait()
        return c

    lax.fori_loop(0, heads, o_wait, 0)

    def g_wait(c, carry):
        pltpu.make_async_copy(newc_ref.at[:, c], newc_ref.at[:, c], gr.at[c]).wait()
        return carry

    lax.fori_loop(0, n_ctx, g_wait, 0)

    def home_sent(h, c):
        sent_home(h, v_src(h), v_dst(me), vs, vr)
        sent_home(h, kst.at[h], k_dst(me), ks, kr)
        sent_home(h, q_src(h), qbuf.at[z], qs, qr)
        return c

    lax.fori_loop(0, heads, home_sent, 0)

    def ctx_sent(i, c):
        other = lax.rem(col + i, n_ctx)
        x_copy(other).wait_send()
        g_copy(other).wait_send()
        return c

    lax.fori_loop(1, n_ctx, ctx_sent, 0)

    def clu_sent(i, c):
        o = lax.rem(me + i, n_clu)
        z_copy(o).wait_send()
        f_copy(o).wait_send()
        return c

    lax.fori_loop(1, n_clu, clu_sent, 0)


def local(n_ctx, n_clu, queries, keys, values, clusters, centroids):
    tok, width = queries.shape
    heads = width // D
    n_z = n_clu // 2
    vmem = pl.BlockSpec(memory_space=pltpu.VMEM)
    hbm = pl.BlockSpec(memory_space=pl.ANY)
    dma = pltpu.SemaphoreType.DMA
    attended, fresh = pl.pallas_call(
        functools.partial(kernel, n_ctx, n_clu),
        out_shape=(
            jax.ShapeDtypeStruct((tok, width), BF),
            jax.ShapeDtypeStruct((n_clu, n_ctx, heads, D), F32),
        ),
        in_specs=[vmem] * 5,
        out_specs=(hbm, hbm),
        scratch_shapes=[
            pltpu.VMEM((heads, D + 16, tok), BF),
            pltpu.VMEM((heads, tok, 2 * D), BF),
            pltpu.VMEM((n_clu, 2 * D, tok), BF),
            pltpu.VMEM((n_clu, tok, 2 * D), BF),
            pltpu.VMEM((n_z, tok, D), BF),
            pltpu.VMEM((n_z, tok, D), BF),
            pltpu.VMEM((tok, 2 * D), F32),
            pltpu.VMEM((n_ctx, heads, n_clu, D), BF),
            pltpu.VMEM((n_ctx, heads, n_clu, D), BF),
            pltpu.VMEM((n_clu * heads, D), F32),
            pltpu.VMEM((n_clu, heads, D), F32),
            pltpu.VMEM((n_clu, heads, D), F32),
            dma((heads,)),
            dma((n_z,)),
            dma((heads,)),
            dma((n_z,)),
            dma((heads,)),
            dma((n_z,)),
            dma((n_z,)),
            dma((n_z,)),
            dma((n_z,)),
            dma((n_z,)),
            dma((n_z,)),
            dma((heads,)),
            dma((n_ctx,)),
            dma((n_ctx,)),
            dma((n_clu,)),
            dma((n_clu,)),
            dma((n_clu,)),
            dma((n_clu,)),
            dma((n_ctx,)),
            dma((n_ctx,)),
        ],
        compiler_params=pltpu.CompilerParams(
            collective_id=0, has_side_effects=True, vmem_limit_bytes=40 * 1024 * 1024
        ),
        cost_estimate=pl.CostEstimate(
            flops=2 * 2 * 2 * D * tok * tok * n_clu * n_clu // 4,
            bytes_accessed=8 * tok * width,
            transcendentals=tok * tok * n_clu * n_clu // 4,
        ),
    )(queries, keys, values, clusters.T, centroids)
    return attended, fresh.reshape(n_clu * n_ctx, heads, D)


def solution(mesh):
    placed = (
        P(("ctx", "clu"), None),
        P(("ctx", "clu"), None),
        P(("ctx", "clu"), None),
        P(("ctx", "clu"), None),
        P("clu", None, None),
    )
    return jax.shard_map(
        functools.partial(local, mesh.shape["ctx"], mesh.shape["clu"]),
        mesh=mesh,
        in_specs=placed,
        out_specs=(P(("ctx", "clu"), None), P()),
        check_vma=False,
    )
```

time: 605 us -> 220 us (0.36)
  waiting for transfers between devices: 363 us -> 0 us
  Pallas kernels: 0 us -> 213 us
  blocking collectives: 63.7 us -> 0 us
  local copies, waits for them, and re-layouts: 53.7 us -> 6.77 us
  starting transfers between devices: 44.4 us -> 0 us
  other arithmetic: 37.2 us -> 0 us
  matrix products: 27.3 us -> 0 us
  between operations: 14.4 us -> 0.65 us
    all_to_all x5 -> x0, waiting for transfers between devices: 283 us -> none  [the longest x1 97.9 us: local(): lax.all_to_all(packed[2], 'clu', split_axis=0, concat_axis=0, tiled=True)]
    pallas_call x0 -> x1, Pallas kernels: none -> 213 us  [local(): pl.pallas_call(functools.partial(kernel, n_ctx, n_clu), out_shape=(jax.Sh...]
    all_gather x1 -> x0, waiting for transfers between devices: 80 us -> none  [local(): gathered = lax.all_gather(fresh, 'clu', axis=0, tiled=True)]
    psum x1 -> x0, blocking collectives: 63.7 us -> none  [local(): total = lax.psum(sums.astype(jnp.bfloat16), 'ctx').astype(jnp.float32)]
    all_to_all x5 -> x0, starting transfers between devices: 44.4 us -> none  [the longest x1 16.7 us: local(): lax.all_to_all(packed[3], 'clu', split_axis=0, concat_axis=0, tiled=True)]
    dot_general x32 -> x0, matrix products: 27.3 us -> none  [the longest x8 13.6 us: attend_one(): jnp.dot(probs, value_rows, preferred_element_type=jnp.float32)]
    another operation x2 -> x0, other arithmetic: 18.1 us -> none
    unnamed x7 -> x0, other arithmetic: 16 us -> none
  transfers between devices with their start and end apart: 6 -> 0, of which waited for: 5 -> 0; matrix products, arithmetic and copies ran while one was open for 4% -> 0% of each run, Pallas kernels for 0% -> 0%
where the time goes in v1:
time: 220 us
  Pallas kernels  213 us (97%)
  local copies, waits for them, and re-layouts  6.77 us (3%)
    pallas_call x1, Pallas kernels, local(): pl.pallas_call(functools.partial(kernel, n_ctx, n_clu), out_shape=(jax.Sh...  213 us
    unnamed x12, local copies, waits for them, and re-layouts  6.77 us

profile of v1, /device:TPU:1, one launch (start us, length us, event | category | flops | bytes accessed | tf_op | source)
XLA Modules:
  0.0 220.0 jit_solution(10466961861620970028)
XLA Ops:
  0.6 0.0 copy-start
  0.6 1.0 copy-done
  1.7 0.0 copy-start.1
  1.7 1.0 copy-done.1
  2.7 0.0 copy-start.2
  2.7 1.0 copy-done.2
  3.8 0.0 copy-start.3
  3.8 0.8 copy-done.3
  4.6 0.0 copy-start.4
  4.6 0.7 copy-done.4
  5.3 212.6 %shard_map.68 = (bf16[256,1024]{1,0:T(8,128)(2,1)S(1)}, f32[32,16,8,128]{3,2,1,0:T(8,128)S(1)}) custom-call(bf16[256,1024]{1,0:T(8,128)(2,1)S(1)} %copy-done, bf16[256,1024]{1,0:T(8,128)(2,1)S(1)} %copy-done.1, bf16[256,1024]{1,0:T(8,128)(2,1)S(1)} %copy-done.2, s32[8,256]{1,0:T(8,128)S(1)} %bitcast.3, f32[16,8,128]{2,1,0:T(8,128)S(1)} %copy-done.3), custom_call_target="tpu_custom_call" | custom-call | flops 17179869184 | bytes 2097152 | tf_op jit(solution)/shard_map/pallas_call | solution.py:408
  217.9 0.8 copy.9
  218.7 1.3 copy.10
Async XLA Ops:
  0.6 1.0 copy-start
  1.7 1.0 copy-start.1
  2.7 1.0 copy-start.2
  3.8 0.8 copy-start.3
  4.6 0.7 copy-start.4

commit v2 on v1

--- a/solution.py
+++ b/solution.py
@@ -34,6 +34,10 @@
     cent_ref,
     out_ref,
     newc_ref,
+    qin,
+    kin,
+    ids,
+    cen,
     kst,
     nrm,
     kbuf,
@@ -46,6 +50,8 @@
     zst,
     zin,
     fin,
+    fnb,
+    ls,
     vs,
     vr,
     ks,
@@ -82,7 +88,8 @@
     my_head = z // step
 
     def spread(i, base, n):
-        off = jnp.where(lax.rem(i, 2) == 1, (i + 1) // 2, n - i // 2)
+        j = n - 1 - i
+        off = jnp.where(lax.rem(j, 2) == 1, (j + 1) // 2, n - j // 2)
         return lax.rem(base + off, n)
 
     def remote(src, dst, send, recv, dev):
@@ -103,6 +110,12 @@
         pl.semaphore_signal(barrier, inc=1, device_id=(lax.rem(col + i, n_ctx), me), device_id_type=MESH)
         return c
 
+    loads = [
+        pltpu.make_async_copy(src, dst, ls.at[i])
+        for i, (src, dst) in enumerate(((k_ref, kin), (q_ref, qin), (clt_ref, ids), (cent_ref, cen)))
+    ]
+    for load in loads:
+        load.start()
     lax.fori_loop(1, n_clu, greet_clu, 0)
     lax.fori_loop(1, n_ctx, greet_ctx, 0)
     pl.semaphore_wait(barrier, n_clu - 1 + n_ctx - 1)
@@ -144,37 +157,44 @@
 
     lax.fori_loop(0, heads, send_v, 0)
 
+    for load in loads:
+        load.wait()
+
     row_id = lax.broadcasted_iota(jnp.int32, (16, tok), 0)
 
-    def send_k(i, c):
+    def ready_head(i, c):
         h = spread(i, z // step, heads)
-        kn = unit(k_ref[:, lanes(h)].astype(F32))
-        qn = unit(q_ref[:, lanes(h)].astype(F32))
+        kn = unit(kin[:, lanes(h)].astype(F32))
+        qn = unit(qin[:, lanes(h)].astype(F32))
         nrm[h, :, pl.ds(0, D)] = qn
         nrm[h, :, pl.ds(D, D)] = kn
         kst[h, pl.ds(0, D), :] = jnp.transpose(kn.astype(F32)).astype(BF)
-        ids = clt_ref[pl.ds(h, 1), :]
-        code = 2 * (lax.shift_right_logical(jnp.broadcast_to(ids, (16, tok)), row_id) & 1) - 1
+        row = jnp.broadcast_to(ids[pl.ds(h, 1), :], (16, tok))
+        code = 2 * (lax.shift_right_logical(row, row_id) & 1) - 1
         code = jnp.where(row_id < bits, code, jnp.where(row_id == bits, 1, 0))
         kst[h, pl.ds(D, 16), :] = code.astype(F32).astype(BF)
+        return c
+
+    lax.fori_loop(0, heads, ready_head, 0)
+
+    def send_k(i, c):
+        h = spread(i, z // step, heads)
         to_home(h, kst.at[h], k_dst(me), ks, kr)
         return c
-
-    lax.fori_loop(0, heads, send_k, 0)
 
     def send_q(i, c):
         h = spread(i, z // step, heads)
         to_home(h, q_src(h), qbuf.at[z], qs, qr)
         return c
 
-    lax.fori_loop(0, heads, send_q, 0)
+    lax.fori_loop(0, heads // 2, send_k, 0)
 
     n_row = n_ctx * n_clu
     sum_row = lax.broadcasted_iota(jnp.int32, (n_row, tok), 0)
 
     def sum_head(h, c):
-        ids = clt_ref[pl.ds(h, 1), :]
-        place = lax.rem(ids, n_ctx) * n_clu + ids // n_ctx
+        row = ids[pl.ds(h, 1), :]
+        place = lax.rem(row, n_ctx) * n_clu + row // n_ctx
         pick = jnp.where(sum_row == place, 1.0, 0.0).astype(BF)
         both = jnp.dot(pick, nrm[h], preferred_element_type=F32)
         both = both[:, :D] + both[:, D:]
@@ -225,43 +245,8 @@
         return c
 
     lax.fori_loop(1, n_clu, z_start, 0)
+    lax.fori_loop(heads // 2, heads, send_k, 0)
     zin[me] = zst[pl.ds(pl.multiple_of(me * heads, heads), heads), :]
-
-    def z_wait(i, c):
-        o = lax.rem(me + i, n_clu)
-        pltpu.make_async_copy(zin.at[o], zin.at[o], zr.at[o]).wait()
-        return c
-
-    lax.fori_loop(1, n_clu, z_wait, 0)
-    total = jnp.sum(zin[...], axis=0)
-    fin[me] = DECAY * cent_ref[col] + (1.0 - DECAY) / 2.0 * total
-
-    def f_copy(o):
-        return remote(fin.at[me], fin.at[me], fs.at[o], fr.at[me], (col, o))
-
-    def f_start(i, c):
-        f_copy(lax.rem(me + i, n_clu)).start()
-        return c
-
-    lax.fori_loop(1, n_clu, f_start, 0)
-
-    def f_wait(i, c):
-        o = lax.rem(me + i, n_clu)
-        pltpu.make_async_copy(fin.at[o], fin.at[o], fr.at[o]).wait()
-        return c
-
-    lax.fori_loop(1, n_clu, f_wait, 0)
-
-    def g_copy(c):
-        return remote(fin, newc_ref.at[:, col], gs.at[c], gr.at[col], (c, me))
-
-    def g_start(i, c):
-        g_copy(lax.rem(col + i, n_ctx)).start()
-        return c
-
-    lax.fori_loop(1, n_ctx, g_start, 0)
-    own_fresh = pltpu.make_async_copy(fin, newc_ref.at[:, col], gr.at[col])
-    own_fresh.start()
 
     def v_pass(t):
         c = 2 * t + core
@@ -270,15 +255,6 @@
     def k_pass(t):
         c = 2 * t + core
         return remote(k_dst(c), k_dst(c), kfs.at[t], kfr.at[t], sib)
-
-    def out_dst(h):
-        return out_ref.at[:, lanes(h)]
-
-    def o_copy(t):
-        return remote(obuf.at[t], out_dst(my_head), os_.at[t], or_.at[my_head], (col, 2 * t + core))
-
-    def own_copy():
-        return pltpu.make_async_copy(obuf.at[z], out_dst(my_head), or_.at[my_head])
 
     @pl.when(is_home)
     def _():
@@ -290,6 +266,27 @@
 
         lax.fori_loop(0, n_z, pass_v, 0)
 
+    def z_wait(i, c):
+        o = lax.rem(me + i, n_clu)
+        pltpu.make_async_copy(zin.at[o], zin.at[o], zr.at[o]).wait()
+        return c
+
+    lax.fori_loop(1, n_clu, z_wait, 0)
+    total = jnp.sum(zin[...], axis=0)
+    fin[me] = DECAY * cen[col] + (1.0 - DECAY) / 2.0 * total
+
+    def f_copy(o):
+        return remote(fin.at[me], fin.at[me], fs.at[o], fr.at[me], (col, o))
+
+    def f_start(i, c):
+        f_copy(lax.rem(me + i, n_clu)).start()
+        return c
+
+    lax.fori_loop(1, n_clu, f_start, 0)
+    lax.fori_loop(0, heads, send_q, 0)
+
+    @pl.when(is_home)
+    def _():
         def pass_k(i, c):
             t = spread(i, z, n_z)
             pltpu.make_async_copy(k_dst(2 * t + core), k_dst(2 * t + core), kr.at[t]).wait()
@@ -298,6 +295,36 @@
 
         lax.fori_loop(0, n_z, pass_k, 0)
 
+    def f_wait(i, c):
+        o = lax.rem(me + i, n_clu)
+        pltpu.make_async_copy(fin.at[o], fin.at[o], fr.at[o]).wait()
+        return c
+
+    lax.fori_loop(1, n_clu, f_wait, 0)
+    fnb[...] = fin[...].reshape(n_clu * heads, D).astype(BF)
+
+    def g_copy(c):
+        return remote(fnb, newc_ref.at[col], gs.at[c], gr.at[col], (c, me))
+
+    def g_start(i, c):
+        g_copy(lax.rem(col + i, n_ctx)).start()
+        return c
+
+    lax.fori_loop(1, n_ctx, g_start, 0)
+    own_fresh = pltpu.make_async_copy(fnb, newc_ref.at[col], gr.at[col])
+    own_fresh.start()
+
+    def out_dst(h):
+        return out_ref.at[:, lanes(h)]
+
+    def o_copy(t):
+        return remote(obuf.at[t], out_dst(my_head), os_.at[t], or_.at[my_head], (col, 2 * t + core))
+
+    def own_copy():
+        return pltpu.make_async_copy(obuf.at[z], out_dst(my_head), or_.at[my_head])
+
+    @pl.when(is_home)
+    def _():
         def arrive(i, c):
             t = spread(i, z, n_z)
             o = 2 * t + 1 - core
@@ -307,46 +334,57 @@
 
         lax.fori_loop(0, n_z, arrive, 0)
 
-        lane = lax.broadcasted_iota(jnp.int32, (tok, D), 1)
+        n_q, n_k = 2, 4
+        lane = lax.broadcasted_iota(jnp.int32, (n_q * tok, D), 1)
         weight = jnp.where(lane < bits, GAP, jnp.where(lane == bits, -GAP * bits, 0.0))
-        key_at = lax.broadcasted_iota(jnp.int32, (tok, tok), 1)
-        query_at = lax.broadcasted_iota(jnp.int32, (tok, tok), 0) + core * tok
+        key_at = lax.broadcasted_iota(jnp.int32, (n_q * tok, tok), 1)
+        row_at = lax.broadcasted_iota(jnp.int32, (n_q * tok, tok), 0)
+        query_at = (2 * (row_at // tok) + core) * tok + lax.rem(row_at, tok)
 
         def attend(i, carry):
-            t = spread(i, z, n_z)
-            pltpu.make_async_copy(qbuf.at[t], qbuf.at[t], qr.at[t]).wait()
-            mine = qbuf[t].astype(F32) * SCALE
-            code = jnp.transpose(kbuf[2 * t + core, pl.ds(D, D), :].astype(F32)) * weight
+            s = spread(i, z // n_q, n_z // n_q)
+            codes = []
+            for j in range(n_q):
+                t = n_q * s + j
+                pltpu.make_async_copy(qbuf.at[t], qbuf.at[t], qr.at[t]).wait()
+                codes.append(jnp.transpose(kbuf[2 * t + core, pl.ds(D, D), :].astype(F32)))
+            mine = qbuf[pl.ds(n_q * s, n_q)].reshape(n_q * tok, D).astype(F32) * SCALE
+            code = jnp.concatenate(codes, axis=0) * weight
             query = jnp.concatenate([mine, code], axis=1).astype(BF)
 
-            def scores(c):
-                return jnp.exp(jnp.dot(query, kbuf[c], preferred_element_type=F32))
-
-            def mix(p, c):
-                return jnp.dot(p.astype(BF), vbuf[c], preferred_element_type=F32)
-
-            p0 = jnp.where(key_at <= query_at, scores(2 * t), 0.0)
-            p1 = jnp.where(key_at + tok <= query_at, scores(2 * t + 1), 0.0)
-            acc[...] = mix(p0, 2 * t) + mix(p1, 2 * t + 1)
+            def mix(u, last):
+                parts = []
+                for j in range(n_k):
+                    p = jnp.exp(jnp.dot(query, kbuf[n_k * u + j], preferred_element_type=F32))
+                    if last:
+                        p = jnp.where(key_at + j * tok <= query_at, p, 0.0)
+                    parts.append(p.astype(BF))
+                held = vbuf[pl.ds(n_k * u, n_k)].reshape(n_k * tok, 2 * D)
+                return jnp.dot(jnp.concatenate(parts, axis=1), held, preferred_element_type=F32)
+
+            acc[...] = mix(s, True)
 
             def earlier(u, c):
-                acc[...] += mix(scores(2 * u), 2 * u) + mix(scores(2 * u + 1), 2 * u + 1)
+                acc[...] += mix(u, False)
                 return c
 
-            lax.fori_loop(0, t, earlier, 0)
-            obuf[t] = (acc[:, pl.ds(0, D)] / acc[:, pl.ds(D, D)]).astype(BF)
-
-            @pl.when(t == z)
-            def _():
-                own_copy().start()
-
-            @pl.when(t != z)
-            def _():
-                o_copy(t).start()
+            lax.fori_loop(0, s, earlier, 0)
+            mixed = (acc[:, pl.ds(0, D)] / acc[:, pl.ds(D, D)]).astype(BF)
+            obuf[pl.ds(n_q * s, n_q)] = mixed.reshape(n_q, tok, D)
+            for j in range(n_q):
+                t = n_q * s + j
+
+                @pl.when(t == z)
+                def _():
+                    own_copy().start()
+
+                @pl.when(t != z)
+                def _():
+                    o_copy(t).start()
 
             return carry
 
-        lax.fori_loop(0, n_z, attend, 0)
+        lax.fori_loop(0, n_z // n_q, attend, 0)
 
         def done(i, c):
             t = lax.rem(z + i, n_z)
@@ -368,7 +406,7 @@
     lax.fori_loop(0, heads, o_wait, 0)
 
     def g_wait(c, carry):
-        pltpu.make_async_copy(newc_ref.at[:, c], newc_ref.at[:, c], gr.at[c]).wait()
+        pltpu.make_async_copy(newc_ref.at[c], newc_ref.at[c], gr.at[c]).wait()
         return carry
 
     lax.fori_loop(0, n_ctx, g_wait, 0)
@@ -402,30 +440,35 @@
     tok, width = queries.shape
     heads = width // D
     n_z = n_clu // 2
-    vmem = pl.BlockSpec(memory_space=pltpu.VMEM)
     hbm = pl.BlockSpec(memory_space=pl.ANY)
     dma = pltpu.SemaphoreType.DMA
     attended, fresh = pl.pallas_call(
         functools.partial(kernel, n_ctx, n_clu),
         out_shape=(
             jax.ShapeDtypeStruct((tok, width), BF),
-            jax.ShapeDtypeStruct((n_clu, n_ctx, heads, D), F32),
+            jax.ShapeDtypeStruct((n_ctx, n_clu * heads, D), BF),
         ),
-        in_specs=[vmem] * 5,
+        in_specs=[hbm] * 5,
         out_specs=(hbm, hbm),
         scratch_shapes=[
+            pltpu.VMEM((tok, width), BF),
+            pltpu.VMEM((tok, width), BF),
+            pltpu.VMEM((heads, tok), jnp.int32),
+            pltpu.VMEM((n_ctx, heads, D), F32),
             pltpu.VMEM((heads, D + 16, tok), BF),
             pltpu.VMEM((heads, tok, 2 * D), BF),
             pltpu.VMEM((n_clu, 2 * D, tok), BF),
             pltpu.VMEM((n_clu, tok, 2 * D), BF),
             pltpu.VMEM((n_z, tok, D), BF),
             pltpu.VMEM((n_z, tok, D), BF),
-            pltpu.VMEM((tok, 2 * D), F32),
+            pltpu.VMEM((2 * tok, 2 * D), F32),
             pltpu.VMEM((n_ctx, heads, n_clu, D), BF),
             pltpu.VMEM((n_ctx, heads, n_clu, D), BF),
             pltpu.VMEM((n_clu * heads, D), F32),
             pltpu.VMEM((n_clu, heads, D), F32),
             pltpu.VMEM((n_clu, heads, D), F32),
+            pltpu.VMEM((n_clu * heads, D), BF),
+            dma((4,)),
             dma((heads,)),
             dma((n_z,)),
             dma((heads,)),
@@ -456,6 +499,7 @@
             transcendentals=tok * tok * n_clu * n_clu // 4,
         ),
     )(queries, keys, values, clusters.T, centroids)
+    fresh = jnp.swapaxes(fresh.reshape(n_ctx, n_clu, heads, D), 0, 1).astype(F32)
     return attended, fresh.reshape(n_clu * n_ctx, heads, D)
 
 

time: 220 us -> 165 us (0.75)
  the two profiles are of different devices: /device:TPU:1 before, /device:TPU:38 now
where the time goes in v2:
time: 165 us
  Pallas kernels  157 us (95%)
  local copies, waits for them, and re-layouts  7.02 us (4%)
    pallas_call x1, Pallas kernels, local(): pl.pallas_call(functools.partial(kernel, n_ctx, n_clu), out_shape=(jax.Sh...  157 us
    unnamed x11, local copies, waits for them, and re-layouts  5.44 us

profile of v2, /device:TPU:38, one launch (start us, length us, event | category | flops | bytes accessed | tf_op | source)
XLA Modules:
  0.0 165.0 jit_solution(7717798152675287927)
XLA Ops:
  0.6 0.0 copy-start
  0.6 1.0 copy-done
  1.7 0.0 copy-start.1
  1.7 1.0 copy-done.1
  2.7 0.0 copy-start.2
  2.7 1.0 copy-done.2
  3.8 0.0 copy-start.3
  3.8 0.8 copy-done.3
  4.6 0.0 copy-start.4
  4.6 0.7 copy-done.4
  5.3 157.1 %shard_map.68 = (bf16[256,1024]{1,0:T(8,128)(2,1)S(1)}, bf16[16,256,128]{2,1,0:T(8,128)(2,1)S(1)}) custom-call(bf16[256,1024]{1,0:T(8,128)(2,1)S(1)} %copy-done, bf16[256,1024]{1,0:T(8,128)(2,1)S(1)} %copy-done.1, bf16[256,1024]{1,0:T(8,128)(2,1)S(1)} %copy-done.2, s32[8,256]{1,0:T(8,128)S(1)} %bitcast.7, f32[16,8,128]{2,1,0:T(8,128)S(1)} %copy-done.3), custom_call_target="tpu_custom_call" | custom-call | flops 17179869184 | bytes 2097152 | tf_op jit(solution)/shard_map/pallas_call | solution.py:445
  162.4 0.2 convert_bitcast_fusion
  162.6 1.6 copy.7
  164.2 0.8 copy.9
Async XLA Ops:
  0.6 1.0 copy-start
  1.7 1.0 copy-start.1
  2.7 1.0 copy-start.2
  3.8 0.8 copy-start.3
  4.6 0.7 copy-start.4

commit v3 on v2

v3 whole, which is shorter than its diff:
```python
import functools
import math

import jax
import jax.numpy as jnp
from jax import lax
from jax.experimental import pallas as pl
from jax.experimental.pallas import tpu as pltpu
from jax.sharding import PartitionSpec as P

MESH = pl.DeviceIdType.MESH
EPS = 1e-06
SCALE = 8.0
DECAY = 0.75
D = 128
GAP = 64.0

BF = jnp.bfloat16
F32 = jnp.float32


def unit(rows):
    factor = lax.rsqrt(jnp.mean(rows * rows, axis=-1, keepdims=True) + EPS) / math.sqrt(D)
    return (rows * factor).astype(BF)


def kernel(
    n_ctx,
    n_clu,
    q_ref,
    k_ref,
    v_ref,
    clt_ref,
    cent_ref,
    out_ref,
    newc_ref,
    qin,
    kin,
    ids,
    cen,
    kst,
    nrm,
    kbuf,
    vbuf,
    qbuf,
    obuf,
    acc,
    sst,
    sin,
    zst,
    zsx,
    zsh,
    zin,
    fin,
    fnb,
    rel,
    relk,
    rr,
    rs,
    ls,
    vs,
    vr,
    ks,
    kr,
    qs,
    qr,
    ps,
    os_,
    or_,
    xs,
    xr,
    hs,
    zs,
    zr,
    fs,
    fr,
    gs,
    gr,
):
    tok = q_ref.shape[0]
    heads = q_ref.shape[1] // D
    n_z = n_clu // 2
    step = n_z // heads
    bits = max(1, (n_ctx * n_clu - 1).bit_length())

    col = lax.axis_index("ctx")
    me = lax.axis_index("clu")
    z = me // 2
    core = lax.rem(me, 2)
    sib = (col, me + 1 - 2 * core)
    is_home = lax.rem(z, step) == 0
    my_head = z // step
    opposite = lax.rem(z + n_z // 2, n_z)
    by_relay = lax.rem(z, 4) == 0
    relay_chip = lax.rem(z + n_z // 2 + 1, n_z)
    relay_from = lax.rem(z + n_z // 2 - 1, n_z)
    relay_to = lax.rem(z + n_z - 1, n_z)
    is_relay = lax.rem(relay_from, 4) == 0

    def spread(i, base, n):
        j = n - 1 - i
        off = jnp.where(lax.rem(j, 2) == 1, (j + 1) // 2, n - j // 2)
        return lax.rem(base + off, n)

    def remote(src, dst, send, recv, dev):
        return pltpu.make_async_remote_copy(
            src_ref=src, dst_ref=dst, send_sem=send, recv_sem=recv, device_id=dev, device_id_type=MESH
        )

    def lanes(h):
        return pl.ds(pl.multiple_of(h * D, D), D)

    def take(ref, sem):
        pltpu.make_async_copy(ref, ref, sem).wait()

    barrier = pltpu.get_barrier_semaphore()

    def greet_clu(i, c):
        pl.semaphore_signal(barrier, inc=1, device_id=(col, lax.rem(me + 2 * i, n_clu)), device_id_type=MESH)
        return c

    def greet_ctx(i, c):
        pl.semaphore_signal(barrier, inc=1, device_id=(lax.rem(col + i, n_ctx), me), device_id_type=MESH)
        return c

    loads = [
        pltpu.make_async_copy(src, dst, ls.at[i])
        for i, (src, dst) in enumerate(((k_ref, kin), (q_ref, qin), (clt_ref, ids), (cent_ref, cen)))
    ]
    for load in loads:
        load.start()
    pl.semaphore_signal(barrier, inc=1, device_id=sib, device_id_type=MESH)
    lax.fori_loop(1, n_z, greet_clu, 0)
    lax.fori_loop(1, n_ctx, greet_ctx, 0)
    pl.semaphore_wait(barrier, n_z + n_ctx - 1)

    def v_src(h):
        return v_ref.at[:, lanes(h)]

    def q_src(h):
        return nrm.at[h, :, pl.ds(0, D)]

    def q_all(n):
        return nrm.at[pl.ds(0, n), :, pl.ds(0, D)]

    def v_dst(c):
        return vbuf.at[c // 2, lax.rem(c, 2), :, pl.ds(0, D)]

    def k_dst(c):
        return kbuf.at[c // 2, lax.rem(c, 2), pl.ds(0, D + 16), :]

    def to_home(src, dst, send, recv, kind, h, start):
        target = h * step
        around = jnp.logical_and(by_relay, target == opposite)

        if start:

            @pl.when(target == z)
            def _():
                pltpu.make_async_copy(src, dst, recv).start()

        @pl.when(around)
        def _():
            held = relk if kind == 1 else rel.at[kind]
            copy = remote(src, held, send, rr.at[kind], (col, relay_chip * 2 + core))
            copy.start() if start else copy.wait_send()

        @pl.when(jnp.logical_and(target != z, jnp.logical_not(around)))
        def _():
            copy = remote(src, dst, send, recv, (col, target * 2 + core))
            copy.start() if start else copy.wait_send()

    def move_v(h, start):
        to_home(v_src(h), v_dst(me), vs.at[h], vr, 0, h, start)

    def move_k(h, start):
        to_home(kst.at[h], k_dst(me), ks.at[h], kr, 1, h, start)

    def move_q(h):
        to_home(q_src(h), qbuf.at[z], qs, qr.at[z], 2, h, True)

    def relay_copy(kind):
        c = 2 * relay_from + core
        held = relk if kind == 1 else rel.at[kind]
        dst, sem = (
            (v_dst(c), vr),
            (k_dst(c), kr),
            (qbuf.at[relay_from], qr.at[relay_from]),
            (out_ref.at[:, lanes(relay_from // step)], or_),
        )[kind]
        return remote(held, dst, rs.at[kind], sem, (col, relay_to * 2 + core))

    def relay(*kinds):
        @pl.when(is_relay)
        def _():
            for kind in kinds:
                held = relk if kind == 1 else rel.at[kind]
                pltpu.make_async_copy(held, held, rr.at[kind]).wait()
                relay_copy(kind).start()

    def send_v(i, c):
        h = spread(i, z // step, heads)
        move_v(h, True)
        return c

    lax.fori_loop(0, heads, send_v, 0)

    for load in loads:
        load.wait()

    row_id = lax.broadcasted_iota(jnp.int32, (16, tok), 0)

    def ready_head(i, c):
        h = spread(i, z // step, heads)
        kn = unit(kin[:, lanes(h)].astype(F32))
        qn = unit(qin[:, lanes(h)].astype(F32))
        nrm[h, :, pl.ds(0, D)] = qn
        nrm[h, :, pl.ds(D, D)] = kn
        kst[h, pl.ds(0, D), :] = jnp.transpose(kn.astype(F32)).astype(BF)
        row = jnp.broadcast_to(ids[pl.ds(h, 1), :], (16, tok))
        code = 2 * (lax.shift_right_logical(row, row_id) & 1) - 1
        code = jnp.where(row_id < bits, code, jnp.where(row_id == bits, 1, 0))
        kst[h, pl.ds(D, 16), :] = code.astype(F32).astype(BF)
        return c

    lax.fori_loop(0, heads, ready_head, 0)

    def send_k(i, c):
        h = spread(i, z // step, heads)
        move_v(h, False)
        move_k(h, True)
        return c

    def send_q(i, c):
        h = spread(i, z // step, heads)
        move_k(h, False)
        move_q(h)
        return c

    n_row = n_ctx * n_clu
    sum_row = lax.broadcasted_iota(jnp.int32, (n_row, tok), 0)

    def sum_head(h, c):
        row = ids[pl.ds(h, 1), :]
        owner = row // n_ctx
        place = lax.rem(row, n_ctx) * n_clu + lax.rem(owner, 2) * n_z + owner // 2
        pick = jnp.where(sum_row == place, 1.0, 0.0).astype(BF)
        both = jnp.dot(pick, nrm[h], preferred_element_type=F32)
        both = both[:, :D] + both[:, D:]
        sst[:, h, :, :] = both.reshape(n_ctx, n_clu, D).astype(BF)
        return c

    lax.fori_loop(0, heads, sum_head, 0)

    def x_copy(c):
        return remote(sst.at[c], sin.at[col], xs, xr, (c, me))

    def x_start(i, c):
        x_copy(lax.rem(col + i, n_ctx)).start()
        return c

    lax.fori_loop(1, n_ctx, x_start, 0)
    sin[col] = sst[col]

    @pl.when(is_home)
    def _():
        def fill(c, carry):
            vbuf[c // 2, lax.rem(c, 2), :, pl.ds(D, D)] = jnp.ones((tok, D), BF)
            kbuf[c // 2, lax.rem(c, 2), pl.ds(D + 16, D - 16), :] = jnp.zeros((D - 16, tok), BF)
            return carry

        lax.fori_loop(0, n_clu, fill, 0)

    lax.fori_loop(0, heads // 2, send_k, 0)
    take(sin.at[pl.ds(0, n_ctx - 1)], xr)
    for h in range(heads):
        part = sin[0, h].astype(F32)
        for c in range(1, n_ctx):
            part = part + sin[c, h].astype(F32)
        zst[pl.ds(h, n_clu, stride=heads), :] = part

    def half(c):
        return pl.ds(pl.multiple_of(c * n_z * heads, n_z * heads), n_z * heads)

    halves = remote(zst.at[half(1 - core)], zsx, hs.at[0], hs.at[1], sib)
    halves.start()
    halves.wait()
    zsh[...] = zst[half(core), :] + zsx[...]

    def z_rows(t):
        return pl.ds(pl.multiple_of(t * heads, heads), heads)

    def z_copy(t):
        return remote(zsh.at[z_rows(t)], zin.at[z], zs, zr, (col, 2 * t + core))

    def z_start(i, c):
        z_copy(lax.rem(z + i, n_z)).start()
        return c

    lax.fori_loop(1, n_z, z_start, 0)
    zin[z] = zsh[z_rows(z), :]
    lax.fori_loop(heads // 2, heads, send_k, 0)

    all_v = vbuf.at[:, core, :, pl.ds(0, D)]
    all_k = kbuf.at[:, core, pl.ds(0, D + 16), :]
    v_pass = remote(all_v, all_v, ps.at[0], ps.at[1], sib)
    k_pass = remote(all_k, all_k, ps.at[2], ps.at[3], sib)

    @pl.when(is_home)
    def _():
        take(all_v, vr)
        v_pass.start()

    relay(0)
    lax.fori_loop(0, heads // 2, send_q, 0)

    take(zin.at[pl.ds(0, n_z - 1)], zr)
    total = jnp.sum(zin[...], axis=0)
    fin[z] = DECAY * cen[col] + (1.0 - DECAY) / 2.0 * total

    def f_copy(t):
        return remote(fin.at[z], fin.at[z], fs, fr, (col, 2 * t + core))

    def f_start(i, c):
        f_copy(lax.rem(z + i, n_z)).start()
        return c

    lax.fori_loop(1, n_z, f_start, 0)
    lax.fori_loop(heads // 2, heads, send_q, 0)

    @pl.when(is_home)
    def _():
        take(all_k, kr)
        k_pass.start()

    relay(1)

    def g_copy(c):
        return remote(fnb, newc_ref.at[core, col], gs, gr, (c, me))

    def g_start(i, c):
        g_copy(lax.rem(col + i, n_ctx)).start()
        return c

    take(fin.at[pl.ds(0, n_z - 1)], fr)
    fnb[...] = fin[...].reshape(n_z * heads, D).astype(BF)
    lax.fori_loop(1, n_ctx, g_start, 0)
    pltpu.make_async_copy(fnb, newc_ref.at[core, col], gr).start()
    g_pass = remote(newc_ref.at[core], newc_ref.at[core], hs.at[2], hs.at[3], sib)

    def share():
        take(newc_ref.at[core], gr)
        g_pass.start()

    relay(2)

    @pl.when(jnp.logical_not(is_home))
    def _():
        share()

    relay(3)

    def out_dst(h):
        return out_ref.at[:, lanes(h)]

    def send_back(t):
        around = jnp.logical_and(by_relay, t == opposite)

        @pl.when(t == z)
        def _():
            pltpu.make_async_copy(obuf.at[t], out_dst(my_head), or_).start()

        @pl.when(around)
        def _():
            copy = remote(obuf.at[t], rel.at[3], os_, rr.at[3], (col, relay_chip * 2 + core))
            copy.start()

        @pl.when(jnp.logical_and(t != z, jnp.logical_not(around)))
        def _():
            copy = remote(obuf.at[t], out_dst(my_head), os_, or_, (col, 2 * t + core))
            copy.start()

    @pl.when(is_home)
    def _():
        v_pass.wait_recv()
        k_pass.wait_recv()

        n_q, n_k = 2, 4
        lane = lax.broadcasted_iota(jnp.int32, (n_q * tok, D), 1)
        weight = jnp.where(lane < bits, GAP, jnp.where(lane == bits, -GAP * bits, 0.0))
        key_at = lax.broadcasted_iota(jnp.int32, (n_q * tok, tok), 1)
        row_at = lax.broadcasted_iota(jnp.int32, (n_q * tok, tok), 0)
        query_at = (2 * (row_at // tok) + core) * tok + lax.rem(row_at, tok)

        def attend(i, carry):
            s = spread(i, z // n_q, n_z // n_q)
            codes = []
            for j in range(n_q):
                t = n_q * s + j
                pltpu.make_async_copy(qbuf.at[t], qbuf.at[t], qr.at[t]).wait()
                codes.append(jnp.transpose(kbuf[t, core, pl.ds(D, D), :].astype(F32)))
            mine = qbuf[pl.ds(n_q * s, n_q)].reshape(n_q * tok, D).astype(F32) * SCALE
            code = jnp.concatenate(codes, axis=0) * weight
            query = jnp.concatenate([mine, code], axis=1).astype(BF)

            def mix(u, last):
                parts = []
                for j in range(n_k):
                    p = jnp.exp(jnp.dot(query, kbuf[n_k // 2 * u + j // 2, j % 2], preferred_element_type=F32))
                    if last:
                        p = jnp.where(key_at + j * tok <= query_at, p, 0.0)
                    parts.append(p.astype(BF))
                held = vbuf[pl.ds(n_k // 2 * u, n_k // 2)].reshape(n_k * tok, 2 * D)
                return jnp.dot(jnp.concatenate(parts, axis=1), held, preferred_element_type=F32)

            acc[...] = mix(s, True)

            def earlier(u, c):
                acc[...] += mix(u, False)
                return c

            lax.fori_loop(0, s, earlier, 0)
            mixed = (acc[:, pl.ds(0, D)] / acc[:, pl.ds(D, D)]).astype(BF)
            obuf[pl.ds(n_q * s, n_q)] = mixed.reshape(n_q, tok, D)
            for j in range(n_q):
                send_back(n_q * s + j)

            @pl.when(i == n_z // n_q // 2)
            def _():
                share()

            return carry

        lax.fori_loop(0, n_z // n_q, attend, 0)

        v_pass.wait_send()
        k_pass.wait_send()
        take(obuf.at[pl.ds(0, n_z - 1)], os_)
        take(q_all(heads - 1), qs)

    @pl.when(jnp.logical_not(is_home))
    def _():
        take(q_all(heads), qs)

    @pl.when(is_relay)
    def _():
        for kind in range(4):
            relay_copy(kind).wait_send()

    take(sst.at[pl.ds(0, n_ctx - 1)], xs)
    take(zin.at[pl.ds(0, n_z - 1)], zs)
    take(fin.at[pl.ds(0, n_z - 1)], fs)
    take(newc_ref.at[core, pl.ds(0, n_ctx - 1)], gs)
    g_pass.wait()
    take(out_ref, or_)


def local(n_ctx, n_clu, queries, keys, values, clusters, centroids):
    tok, width = queries.shape
    heads = width // D
    n_z = n_clu // 2
    hbm = pl.BlockSpec(memory_space=pl.ANY)
    dma = pltpu.SemaphoreType.DMA
    attended, fresh = pl.pallas_call(
        functools.partial(kernel, n_ctx, n_clu),
        out_shape=(
            jax.ShapeDtypeStruct((tok, width), BF),
            jax.ShapeDtypeStruct((2, n_ctx, n_z * heads, D), BF),
        ),
        in_specs=[hbm] * 5,
        out_specs=(hbm, hbm),
        scratch_shapes=[
            pltpu.VMEM((tok, width), BF),
            pltpu.VMEM((tok, width), BF),
            pltpu.VMEM((heads, tok), jnp.int32),
            pltpu.VMEM((n_ctx, heads, D), F32),
            pltpu.VMEM((heads, D + 16, tok), BF),
            pltpu.VMEM((heads, tok, 2 * D), BF),
            pltpu.VMEM((n_z, 2, 2 * D, tok), BF),
            pltpu.VMEM((n_z, 2, tok, 2 * D), BF),
            pltpu.VMEM((n_z, tok, D), BF),
            pltpu.VMEM((n_z, tok, D), BF),
            pltpu.VMEM((2 * tok, 2 * D), F32),
            pltpu.VMEM((n_ctx, heads, n_clu, D), BF),
            pltpu.VMEM((n_ctx, heads, n_clu, D), BF),
            pltpu.VMEM((n_clu * heads, D), F32),
            pltpu.VMEM((n_z * heads, D), F32),
            pltpu.VMEM((n_z * heads, D), F32),
            pltpu.VMEM((n_z, heads, D), F32),
            pltpu.VMEM((n_z, heads, D), F32),
            pltpu.VMEM((n_z * heads, D), BF),
            pltpu.VMEM((4, tok, D), BF),
            pltpu.VMEM((D + 16, tok), BF),
            dma((4,)),
            dma((4,)),
            dma((4,)),
            dma((heads,)),
            dma(()),
            dma((heads,)),
            dma(()),
            dma(()),
            dma((n_z,)),
            dma((4,)),
            dma(()),
            dma(()),
            dma(()),
            dma(()),
            dma((4,)),
            dma(()),
            dma(()),
            dma(()),
            dma(()),
            dma(()),
            dma(()),
        ],
        compiler_params=pltpu.CompilerParams(
            collective_id=0, has_side_effects=True, vmem_limit_bytes=60 * 1024 * 1024
        ),
        cost_estimate=pl.CostEstimate(
            flops=2 * 2 * 2 * D * tok * tok * n_clu * n_clu // 4,
            bytes_accessed=8 * tok * width,
            transcendentals=tok * tok * n_clu * n_clu // 4,
        ),
    )(queries, keys, values, clusters.T, centroids)
    fresh = jnp.transpose(fresh.reshape(2, n_ctx, n_z, heads, D), (2, 0, 1, 3, 4)).astype(F32)
    return attended, fresh.reshape(n_clu * n_ctx, heads, D)


def solution(mesh):
    placed = (
        P(("ctx", "clu"), None),
        P(("ctx", "clu"), None),
        P(("ctx", "clu"), None),
        P(("ctx", "clu"), None),
        P("clu", None, None),
    )
    return jax.shard_map(
        functools.partial(local, mesh.shape["ctx"], mesh.shape["clu"]),
        mesh=mesh,
        in_specs=placed,
        out_specs=(P(("ctx", "clu"), None), P()),
        check_vma=False,
    )
```

time: 165 us -> 143 us (0.87)
  the two profiles are of different devices: /device:TPU:38 before, /device:TPU:1 now
where the time goes in v3:
time: 143 us; the launch traced here: 140 us
  Pallas kernels  136 us (95%)
  local copies, waits for them, and re-layouts  2.37 us (2%)
  other arithmetic  1.45 us (1%)
    pallas_call x1, Pallas kernels, local(): pl.pallas_call(functools.partial(kernel, n_ctx, n_clu), out_shape=(jax.Sh...  136 us

profile of v3, /device:TPU:1, one launch (start us, length us, event | category | flops | bytes accessed | tf_op | source)
XLA Modules:
  0.0 140.1 jit_solution(5073207178390561631)
XLA Ops:
  0.6 135.6 %shard_map.68 = (bf16[256,1024]{1,0:T(8,128)(2,1)}, bf16[2,16,128,128]{3,2,1,0:T(8,128)(2,1)}) custom-call(bf16[256,1024]{1,0:T(8,128)(2,1)} %q_ref.1, bf16[256,1024]{1,0:T(8,128)(2,1)} %k_ref.1, bf16[256,1024]{1,0:T(8,128)(2,1)} %v_ref.1, s32[8,256]{1,0:T(8,128)} %bitcast.8, f32[16,8,128]{2,1,0:T(8,128)} %cent_ref.1), custom_call_target="tpu_custom_call" | custom-call | flops 17179869184 | bytes 2097152 | tf_op jit(solution)/shard_map/pallas_call | solution.py:464
  136.3 1.5 %convert_bitcast_fusion = f32[16,2,16,8,128]{4,3,0,2,1:T(8,128)S(1)} fusion(bf16[2,16,128,128]{3,2,1,0:T(8,128)(2,1)} %get-tuple-element.5), kind=kLoop, calls=%fused_computation | loop fusion | flops 524288 | bytes 3145728 | tf_op jit(solution)/shard_map/reshape | solution.py:526
  137.7 0.0 copy-start
  137.8 1.6 %copy.7 = f32[16,2,16,8,128]{4,3,2,1,0:T(8,128)} copy(f32[16,2,16,8,128]{4,3,0,2,1:T(8,128)S(1)} %convert_bitcast_fusion) | data formatting | bytes 4194304 | tf_op jit(solution)/shard_map/reshape | solution.py:526
  139.3 0.0 copy-done
  139.3 0.8 copy.9
Async XLA Ops:
  137.7 1.6 %copy-start = (bf16[256,1024]{1,0:T(8,128)(2,1)S(1)}, bf16[256,1024]{1,0:T(8,128)(2,1)}, u32[]{:S(2)}) copy-start(bf16[256,1024]{1,0:T(8,128)(2,1)} %get-tuple-element.8) | copy-start | bytes 1572868

commit v4 on v3

--- a/solution.py
+++ b/solution.py
@@ -333,7 +333,7 @@
         take(all_k, kr)
         k_pass.start()
 
-    relay(1)
+    relay(1, 2)
 
     def g_copy(c):
         return remote(fnb, newc_ref.at[core, col], gs, gr, (c, me))
@@ -352,8 +352,6 @@
         take(newc_ref.at[core], gr)
         g_pass.start()
 
-    relay(2)
-
     @pl.when(jnp.logical_not(is_home))
     def _():
         share()
@@ -385,7 +383,7 @@
         v_pass.wait_recv()
         k_pass.wait_recv()
 
-        n_q, n_k = 2, 4
+        n_q = 2
         lane = lax.broadcasted_iota(jnp.int32, (n_q * tok, D), 1)
         weight = jnp.where(lane < bits, GAP, jnp.where(lane == bits, -GAP * bits, 0.0))
         key_at = lax.broadcasted_iota(jnp.int32, (n_q * tok, tok), 1)
@@ -393,7 +391,7 @@
         query_at = (2 * (row_at // tok) + core) * tok + lax.rem(row_at, tok)
 
         def attend(i, carry):
-            s = spread(i, z // n_q, n_z // n_q)
+            s = spread(jnp.where(i < 3, lax.rem(i + 1, 3), i), z // n_q, n_z // n_q)
             codes = []
             for j in range(n_q):
                 t = n_q * s + j
@@ -403,23 +401,33 @@
             code = jnp.concatenate(codes, axis=0) * weight
             query = jnp.concatenate([mine, code], axis=1).astype(BF)
 
-            def mix(u, last):
-                parts = []
-                for j in range(n_k):
-                    p = jnp.exp(jnp.dot(query, kbuf[n_k // 2 * u + j // 2, j % 2], preferred_element_type=F32))
-                    if last:
-                        p = jnp.where(key_at + j * tok <= query_at, p, 0.0)
-                    parts.append(p.astype(BF))
-                held = vbuf[pl.ds(n_k // 2 * u, n_k // 2)].reshape(n_k * tok, 2 * D)
+            def weigh(rows, t, c, causal):
+                p = jnp.exp(jnp.dot(query[rows], kbuf[t, c], preferred_element_type=F32))
+                if causal:
+                    p = jnp.where(key_at[rows] + (2 * (t - n_q * s) + c) * tok <= query_at[rows], p, 0.0)
+                return p.astype(BF)
+
+            def mix(rows, t, n, causal):
+                parts = [
+                    weigh(rows, t + k, c, causal and k == n - 1) for k in range(n) for c in range(2)
+                ]
+                held = vbuf[pl.ds(t, n)].reshape(2 * n * tok, 2 * D)
                 return jnp.dot(jnp.concatenate(parts, axis=1), held, preferred_element_type=F32)
 
-            acc[...] = mix(s, True)
+            every = slice(0, n_q * tok)
+            for j in range(n_q):
+                rows = slice(j * tok, (j + 1) * tok)
+                acc[rows, :] = mix(rows, n_q * s, j + 1, True)
+
+            @pl.when(lax.rem(s, 2) == 1)
+            def _():
+                acc[...] += mix(every, n_q * (s - 1), n_q, False)
 
             def earlier(u, c):
-                acc[...] += mix(u, False)
+                acc[...] += mix(every, 2 * n_q * u, 2 * n_q, False)
                 return c
 
-            lax.fori_loop(0, s, earlier, 0)
+            lax.fori_loop(0, s // 2, earlier, 0)
             mixed = (acc[:, pl.ds(0, D)] / acc[:, pl.ds(D, D)]).astype(BF)
             obuf[pl.ds(n_q * s, n_q)] = mixed.reshape(n_q, tok, D)
             for j in range(n_q):

time: 143 us -> 139 us (0.972); the launches traced: 140 us -> 139 us
  no operation moved by 1% of the time
where the time goes in v4:
time: 139 us
  Pallas kernels  135 us (97%)
  local copies, waits for them, and re-layouts  2.37 us (2%)
  other arithmetic  1.45 us (1%)
    pallas_call x1, Pallas kernels, local(): pl.pallas_call(functools.partial(kernel, n_ctx, n_clu), out_shape=(jax.Sh...  135 us

profile of v4, /device:TPU:1, one launch (start us, length us, event | category | flops | bytes accessed | tf_op | source)
XLA Modules:
  0.0 139.1 jit_solution(12113407189480668275)
XLA Ops:
  0.6 134.6 %shard_map.68 = (bf16[256,1024]{1,0:T(8,128)(2,1)}, bf16[2,16,128,128]{3,2,1,0:T(8,128)(2,1)}) custom-call(bf16[256,1024]{1,0:T(8,128)(2,1)} %q_ref.1, bf16[256,1024]{1,0:T(8,128)(2,1)} %k_ref.1, bf16[256,1024]{1,0:T(8,128)(2,1)} %v_ref.1, s32[8,256]{1,0:T(8,128)} %bitcast.8, f32[16,8,128]{2,1,0:T(8,128)} %cent_ref.1), custom_call_target="tpu_custom_call" | custom-call | flops 17179869184 | bytes 2097152 | tf_op jit(solution)/shard_map/pallas_call | solution.py:472
  135.3 1.5 %convert_bitcast_fusion = f32[16,2,16,8,128]{4,3,0,2,1:T(8,128)S(1)} fusion(bf16[2,16,128,128]{3,2,1,0:T(8,128)(2,1)} %get-tuple-element.5), kind=kLoop, calls=%fused_computation | loop fusion | flops 524288 | bytes 3145728 | tf_op jit(solution)/shard_map/reshape | solution.py:534
  136.7 0.0 copy-start
  136.7 1.6 %copy.7 = f32[16,2,16,8,128]{4,3,2,1,0:T(8,128)} copy(f32[16,2,16,8,128]{4,3,0,2,1:T(8,128)S(1)} %convert_bitcast_fusion) | data formatting | bytes 4194304 | tf_op jit(solution)/shard_map/reshape | solution.py:534
  138.3 0.0 copy-done
  138.3 0.8 copy.9
Async XLA Ops:
  136.7 1.6 %copy-start = (bf16[256,1024]{1,0:T(8,128)(2,1)S(1)}, bf16[256,1024]{1,0:T(8,128)(2,1)}, u32[]{:S(2)}) copy-start(bf16[256,1024]{1,0:T(8,128)(2,1)} %get-tuple-element.8) | copy-start | bytes 1572868

commit v5 on v4

--- a/solution.py
+++ b/solution.py
@@ -232,9 +232,7 @@
         return c
 
     def send_q(i, c):
-        h = spread(i, z // step, heads)
-        move_k(h, False)
-        move_q(h)
+        move_q(spread(i, z // step, heads))
         return c
 
     n_row = n_ctx * n_clu
@@ -419,15 +417,15 @@
                 rows = slice(j * tok, (j + 1) * tok)
                 acc[rows, :] = mix(rows, n_q * s, j + 1, True)
 
-            @pl.when(lax.rem(s, 2) == 1)
-            def _():
-                acc[...] += mix(every, n_q * (s - 1), n_q, False)
-
-            def earlier(u, c):
-                acc[...] += mix(every, 2 * n_q * u, 2 * n_q, False)
-                return c
-
-            lax.fori_loop(0, s // 2, earlier, 0)
+            run = 1
+            while run < n_z // n_q:
+
+                @pl.when(lax.rem(s // run, 2) == 1)
+                def _(run=run):
+                    acc[...] += mix(every, n_q * (s // (2 * run)) * 2 * run, n_q * run, False)
+
+                run *= 2
+
             mixed = (acc[:, pl.ds(0, D)] / acc[:, pl.ds(D, D)]).astype(BF)
             obuf[pl.ds(n_q * s, n_q)] = mixed.reshape(n_q, tok, D)
             for j in range(n_q):
@@ -455,6 +453,11 @@
         for kind in range(4):
             relay_copy(kind).wait_send()
 
+    def keys_left(h, c):
+        move_k(h, False)
+        return c
+
+    lax.fori_loop(0, heads, keys_left, 0)
     take(sst.at[pl.ds(0, n_ctx - 1)], xs)
     take(zin.at[pl.ds(0, n_z - 1)], zs)
     take(fin.at[pl.ds(0, n_z - 1)], fs)

time: 139 us -> 139 us (level)
  no operation moved by 1% of the time
where the time goes in v5:
time: 139 us
  Pallas kernels  134 us (96%)
  local copies, waits for them, and re-layouts  2.37 us (2%)
  other arithmetic  1.45 us (1%)
    pallas_call x1, Pallas kernels, local(): pl.pallas_call(functools.partial(kernel, n_ctx, n_clu), out_shape=(jax.Sh...  134 us

profile of v5, /device:TPU:1, one launch (start us, length us, event | category | flops | bytes accessed | tf_op | source)
XLA Modules:
  0.0 138.8 jit_solution(18420431269910149813)
XLA Ops:
  0.6 134.4 %shard_map.68 = (bf16[256,1024]{1,0:T(8,128)(2,1)}, bf16[2,16,128,128]{3,2,1,0:T(8,128)(2,1)}) custom-call(bf16[256,1024]{1,0:T(8,128)(2,1)} %q_ref.1, bf16[256,1024]{1,0:T(8,128)(2,1)} %k_ref.1, bf16[256,1024]{1,0:T(8,128)(2,1)} %v_ref.1, s32[8,256]{1,0:T(8,128)} %bitcast.8, f32[16,8,128]{2,1,0:T(8,128)} %cent_ref.1), custom_call_target="tpu_custom_call" | custom-call | flops 17179869184 | bytes 2097152 | tf_op jit(solution)/shard_map/pallas_call | solution.py:475
  135.0 1.5 %convert_bitcast_fusion = f32[16,2,16,8,128]{4,3,0,2,1:T(8,128)S(1)} fusion(bf16[2,16,128,128]{3,2,1,0:T(8,128)(2,1)} %get-tuple-element.5), kind=kLoop, calls=%fused_computation | loop fusion | flops 524288 | bytes 3145728 | tf_op jit(solution)/shard_map/reshape | solution.py:537
  136.5 0.0 copy-start
  136.5 1.6 %copy.7 = f32[16,2,16,8,128]{4,3,2,1,0:T(8,128)} copy(f32[16,2,16,8,128]{4,3,0,2,1:T(8,128)S(1)} %convert_bitcast_fusion) | data formatting | bytes 4194304 | tf_op jit(solution)/shard_map/reshape | solution.py:537
  138.1 0.0 copy-done
  138.1 0.8 copy.9
Async XLA Ops:
  136.5 1.6 %copy-start = (bf16[256,1024]{1,0:T(8,128)(2,1)S(1)}, bf16[256,1024]{1,0:T(8,128)(2,1)}, u32[]{:S(2)}) copy-start(bf16[256,1024]{1,0:T(8,128)(2,1)} %get-tuple-element.8) | copy-start | bytes 1572868
